TPU v7x, 128 devices: a whole 4x4x4 slice. The times are simulated.
128 devices in a mesh: dp: 32 (over y_lo, x, z), tensor: 4 (over y_hi, core).
Axes of the slice: x: 4, y: 4 (y_hi: 2, y_lo: 2; y = y_hi * 2 + y_lo), z: 4, core: 2. Of those that a mesh axis runs over, the one named last changes fastest.
Arguments:
- tokens: bfloat16 [32768, 1024], P(('dp', 'tensor')), may hold values from -6 to 6
- segment_ids: int32 [32768], P('dp'), may hold values from 0 to 510, as said below
- norm_gain: bfloat16 [2, 1024], P(None, ('dp', 'tensor')), may hold values from 0.25 to 1.75
- norm_shift: bfloat16 [2, 1024], P(None, ('dp', 'tensor')), may hold values from -3 to 3
- qkv_weight: bfloat16 [2, 3, 1024, 1024], P(None, None, 'dp', 'tensor'), may hold values from -0.1875 to 0.1875
- proj_weight: bfloat16 [2, 1024, 1024], P(None, ('tensor', 'dp')), may hold values from -1.5 to 1.5
- up_weight: bfloat16 [2, 1024, 4096], P(None, 'dp', 'tensor'), may hold values from -0.1875 to 0.1875
- hidden_bias: bfloat16 [2, 4096], P(None, ('tensor', 'dp')), may hold values from -3 to 3
- down_weight: bfloat16 [2, 4096, 1024], P(None, ('tensor', 'dp')), may hold values from -0.09375 to 0.09375
- final_bias: bfloat16 [2, 1024], P(None, ('dp', 'tensor')), may hold values from -3 to 3
- cotangent: bfloat16 [32768, 1024], P(('dp', 'tensor')), may hold values from -6 to 6
Outputs:
- mixed: bfloat16 [32768, 1024], P(('dp', 'tensor'))
- token_grad: float32 [32768, 1024], P(('dp', 'tensor'))
- gain_grad: float32 [2, 1024], P(None, ('dp', 'tensor'))
- shift_grad: float32 [2, 1024], P(None, ('dp', 'tensor'))
- qkv_grad: float32 [2, 3, 1024, 1024], P(None, None, 'dp', 'tensor')
- proj_grad: float32 [2, 1024, 1024], P(None, ('tensor', 'dp'))
- up_grad: float32 [2, 1024, 4096], P(None, 'dp', 'tensor')
- hidden_grad: float32 [2, 4096], P(None, ('tensor', 'dp'))
- down_grad: float32 [2, 4096, 1024], P(None, ('tensor', 'dp'))
- final_grad: float32 [2, 1024], P(None, ('dp', 'tensor'))
Inputs may be any that keep to these rules, and one draw needn't show every extreme that they name: `segment_ids`: within each group of 1024 consecutive tokens the ids start at 0 and never fall; a sequence holds 1 to 1024 tokens; some group reaches the largest id.
All inputs are finite; a program needn't handle non-finite values.
Results may differ from a plain program's by a relative error of at most 0.028.
Values may be sent and summed in bfloat16 or wider, within the bound.
A program may use at most 192 MiB of HBM per device.

v0:
```python
import math

import jax
import jax.numpy as jnp
from jax import lax
from jax.sharding import PartitionSpec as P

HEAD_DIM = 64
ROT = 32


epsilon = 1e-05
block_rows = 512


def seq_positions(segments):
    count = segments.shape[0]
    index = jnp.arange(count, dtype=jnp.int32)
    first = jnp.concatenate([jnp.ones((1,), dtype=bool), segments[1:] != segments[:-1]])
    begin = lax.cummax(jnp.where(first, index, 0), axis=0)
    return index - begin


def rotary_tables(positions):
    half = ROT // 2
    freq = jnp.exp(jnp.arange(half, dtype=jnp.float32) * (-2.0 * math.log(10000.0) / ROT))
    angle = positions.astype(jnp.float32)[:, None] * freq[None, :]
    return (jnp.cos(angle)[:, None, :], jnp.sin(angle)[:, None, :])


def rotate(heads, cosine, sine):
    half = ROT // 2
    first = heads[..., :half]
    second = heads[..., half:ROT]
    return jnp.concatenate(
        [first * cosine - second * sine, second * cosine + first * sine, heads[..., ROT:]], axis=-1
    )


def contract_rows(left, right):
    return lax.dot_general(
        left, right, (((0,), (0,)), ((), ())), preferred_element_type=jnp.float32
    )


def contract_cols(left, right):
    return lax.dot_general(
        left, right, (((1,), (1,)), ((), ())), preferred_element_type=jnp.float32
    )


def masked_scores(query, keys, segments, start, size, stop):
    index = jnp.arange(segments.shape[0], dtype=jnp.int32)
    own_ids = segments[start : start + size]
    allowed = (own_ids[:, None] == segments[None, :stop]) & (
        index[start : start + size, None] >= index[None, :stop]
    )
    scale = query.shape[-1] ** (-0.5)
    scores = (
        jnp.einsum(
            "qhe,khe->hqk",
            query[start : start + size],
            keys[:stop],
            preferred_element_type=jnp.float32,
        )
        * scale
    )
    return jnp.where(allowed[None], scores, -1e30)


def attend_forward(query, keys, values, segments):
    count = query.shape[0]
    size = min(block_rows, count)
    outputs = []
    totals = []
    for block in range(count // size):
        start = block * size
        stop = start + size
        scores = masked_scores(query, keys, segments, start, size, stop)
        peak = jnp.max(scores, axis=-1, keepdims=True)
        weights = jnp.exp(scores - peak)
        total = jnp.sum(weights, axis=-1, keepdims=True)
        probs = (weights / total).astype(jnp.bfloat16)
        outputs.append(
            jnp.einsum("hqk,khe->qhe", probs, values[:stop], preferred_element_type=jnp.float32)
        )
        totals.append(peak + jnp.log(total))
    return (jnp.concatenate(outputs, axis=0), jnp.concatenate(totals, axis=1))


def attend_backward(query, keys, values, segments, logsum, grad_out):
    count = query.shape[0]
    size = min(block_rows, count)
    scale = query.shape[-1] ** (-0.5)
    grad_keys = jnp.zeros(keys.shape, jnp.float32)
    grad_values = jnp.zeros(values.shape, jnp.float32)
    grad_rows = []
    for block in range(count // size):
        start = block * size
        stop = start + size
        scores = masked_scores(query, keys, segments, start, size, stop)
        probs = jnp.exp(scores - logsum[:, start:stop])
        probs_low = probs.astype(jnp.bfloat16)
        grad_block = grad_out[start:stop]
        grad_values = grad_values.at[:stop].add(
            jnp.einsum("hqk,qhe->khe", probs_low, grad_block, preferred_element_type=jnp.float32)
        )
        grad_probs = jnp.einsum(
            "qhe,khe->hqk", grad_block, values[:stop], preferred_element_type=jnp.float32
        )
        delta = jnp.sum(probs * grad_probs, axis=-1, keepdims=True)
        grad_scores = (probs * (grad_probs - delta)).astype(jnp.bfloat16)
        grad_rows.append(
            jnp.einsum("hqk,khe->qhe", grad_scores, keys[:stop], preferred_element_type=jnp.float32)
            * scale
        )
        grad_keys = grad_keys.at[:stop].add(
            jnp.einsum(
                "hqk,qhe->khe", grad_scores, query[start:stop], preferred_element_type=jnp.float32
            )
            * scale
        )
    return (jnp.concatenate(grad_rows, axis=0), grad_keys, grad_values)


def layer_forward(state, gain, shift, weights, bias_final, segments, cosine, sine):
    qkv_full, proj_full, up_full, hidden_full, down_full = weights
    center = state - jnp.mean(state, axis=-1, keepdims=True)
    inverse = lax.rsqrt(jnp.mean(center * center, axis=-1, keepdims=True) + epsilon)
    unit = center * inverse
    normed_own = (unit * gain + shift).astype(jnp.bfloat16)
    normed = lax.all_gather(normed_own, "tensor", axis=0, tiled=True)
    count = normed.shape[0]
    joined = jnp.einsum("td,cde->cte", normed, qkv_full, preferred_element_type=jnp.float32)
    joined = joined.reshape(3, count, -1, HEAD_DIM)
    query = rotate(joined[0], cosine, sine).astype(jnp.bfloat16)
    keys = rotate(joined[1], cosine, sine).astype(jnp.bfloat16)
    values = joined[2].astype(jnp.bfloat16)
    attended, logsum = attend_forward(query, keys, values, segments)
    attended = attended.astype(jnp.bfloat16).reshape(count, -1)
    up = jnp.dot(normed, up_full, preferred_element_type=jnp.float32) + hidden_full.astype(
        jnp.float32
    )
    active = jax.nn.gelu(up, approximate=True).astype(jnp.bfloat16)
    local_sum = jnp.dot(attended, proj_full, preferred_element_type=jnp.float32) + jnp.dot(
        active, down_full, preferred_element_type=jnp.float32
    )
    branch = lax.psum_scatter(local_sum, "tensor", scatter_dimension=0, tiled=True)
    result = state + branch + bias_final
    kept = (unit, inverse, normed, query, keys, values, logsum, attended, up, active)
    return (result, kept)


def layer_backward(grad, gain, weights, kept, segments, cosine, sine):
    qkv_full, proj_full, up_full, hidden_full, down_full = weights
    unit, inverse, normed, query, keys, values, logsum, attended, up, active = kept
    count = normed.shape[0]
    grad_final = jnp.sum(grad, axis=0)
    grad_rows = lax.all_gather(grad.astype(jnp.bfloat16), "tensor", axis=0, tiled=True)
    grad_down = contract_rows(active, grad_rows)
    grad_active = contract_cols(grad_rows, down_full)
    _, gelu_back = jax.vjp(lambda value: jax.nn.gelu(value, approximate=True), up)
    grad_up = gelu_back(grad_active)[0].astype(jnp.bfloat16)
    grad_hidden = jnp.sum(grad_up, axis=0, dtype=jnp.float32)
    grad_upw = contract_rows(normed, grad_up)
    grad_normed = contract_cols(grad_up, up_full)
    grad_proj = contract_rows(attended, grad_rows)
    grad_attended = contract_cols(grad_rows, proj_full).astype(jnp.bfloat16).reshape(query.shape)
    grad_query, grad_keys, grad_values = attend_backward(
        query, keys, values, segments, logsum, grad_attended
    )
    grad_query = rotate(grad_query, cosine, -sine)
    grad_keys = rotate(grad_keys, cosine, -sine)
    grad_joined = (
        jnp.stack([grad_query, grad_keys, grad_values]).reshape(3, count, -1).astype(jnp.bfloat16)
    )
    grad_qkv = jnp.einsum("td,cte->cde", normed, grad_joined, preferred_element_type=jnp.float32)
    grad_normed = grad_normed + jnp.einsum(
        "cte,cde->td", grad_joined, qkv_full, preferred_element_type=jnp.float32
    )
    grad_own = lax.psum_scatter(
        grad_normed.astype(jnp.bfloat16), "tensor", scatter_dimension=0, tiled=True
    ).astype(jnp.float32)
    grad_gain = jnp.sum(grad_own * unit, axis=0)
    grad_shift = jnp.sum(grad_own, axis=0)
    scaled = grad_own * gain
    grad_state = grad + inverse * (
        scaled
        - jnp.mean(scaled, axis=-1, keepdims=True)
        - unit * jnp.mean(scaled * unit, axis=-1, keepdims=True)
    )
    return (
        grad_state,
        (grad_qkv, grad_proj, grad_upw, grad_hidden, grad_down),
        (grad_gain, grad_shift, grad_final),
    )


def local(
    tokens,
    segment_ids,
    norm_gain,
    norm_shift,
    qkv_weight,
    proj_weight,
    up_weight,
    hidden_bias,
    down_weight,
    final_bias,
    cotangent,
):
    layers = qkv_weight.shape[0]
    gains, shifts, finals = (
        lax.all_gather(norm_gain, ("dp", "tensor"), axis=1, tiled=True),
        lax.all_gather(norm_shift, ("dp", "tensor"), axis=1, tiled=True),
        lax.all_gather(final_bias, ("dp", "tensor"), axis=1, tiled=True),
    )
    gains = gains.astype(jnp.float32)
    shifts = shifts.astype(jnp.float32)
    finals = finals.astype(jnp.float32)
    positions = seq_positions(segment_ids)
    cosine, sine = rotary_tables(positions)
    state = tokens.astype(jnp.float32)
    saved = []
    held = []
    for layer in range(layers):
        weights = (
            lax.all_gather(qkv_weight[layer], "dp", axis=1, tiled=True),
            lax.all_gather(proj_weight[layer], "dp", axis=0, tiled=True),
            lax.all_gather(up_weight[layer], "dp", axis=0, tiled=True),
            lax.all_gather(hidden_bias[layer], "dp", axis=0, tiled=True),
            lax.all_gather(down_weight[layer], "dp", axis=0, tiled=True),
        )
        state, kept = layer_forward(
            state, gains[layer], shifts[layer], weights, finals[layer], segment_ids, cosine, sine
        )
        saved.append(kept)
        held.append(weights)
    mixed = state.astype(jnp.bfloat16)
    grad = cotangent.astype(jnp.float32)
    weight_terms = [None] * layers
    norm_terms = [None] * layers
    for layer in reversed(range(layers)):
        weights = (
            lax.all_gather(qkv_weight[layer], "dp", axis=1, tiled=True),
            lax.all_gather(proj_weight[layer], "dp", axis=0, tiled=True),
            lax.all_gather(up_weight[layer], "dp", axis=0, tiled=True),
            lax.all_gather(hidden_bias[layer], "dp", axis=0, tiled=True),
            lax.all_gather(down_weight[layer], "dp", axis=0, tiled=True),
        )
        grad, terms, small = layer_backward(
            grad, gains[layer], weights, saved[layer], segment_ids, cosine, sine
        )
        weight_terms[layer] = (
            lax.psum_scatter(
                terms[0].astype(jnp.bfloat16), "dp", scatter_dimension=1, tiled=True
            ).astype(jnp.float32),
            lax.psum_scatter(
                terms[1].astype(jnp.bfloat16), "dp", scatter_dimension=0, tiled=True
            ).astype(jnp.float32),
            lax.psum_scatter(
                terms[2].astype(jnp.bfloat16), "dp", scatter_dimension=0, tiled=True
            ).astype(jnp.float32),
            lax.psum_scatter(
                terms[3].astype(jnp.bfloat16), "dp", scatter_dimension=0, tiled=True
            ).astype(jnp.float32),
            lax.psum_scatter(
                terms[4].astype(jnp.bfloat16), "dp", scatter_dimension=0, tiled=True
            ).astype(jnp.float32),
        )
        norm_terms[layer] = small
    stacked = tuple(
        (jnp.stack([weight_terms[layer][member] for layer in range(layers)]) for member in range(5))
    )
    norm_stack = tuple(
        (jnp.stack([norm_terms[layer][member] for layer in range(layers)]) for member in range(3))
    )
    grad_gain, grad_shift, grad_final = (
        lax.psum_scatter(norm_stack[0], ("dp", "tensor"), scatter_dimension=1, tiled=True),
        lax.psum_scatter(norm_stack[1], ("dp", "tensor"), scatter_dimension=1, tiled=True),
        lax.psum_scatter(norm_stack[2], ("dp", "tensor"), scatter_dimension=1, tiled=True),
    )
    return (
        mixed,
        grad,
        grad_gain,
        grad_shift,
        stacked[0],
        stacked[1],
        stacked[2],
        stacked[3],
        stacked[4],
        grad_final,
    )


def solution(mesh):
    placed = (
        P(("dp", "tensor"), None),
        P("dp"),
        P(None, ("dp", "tensor")),
        P(None, ("dp", "tensor")),
        P(None, None, "dp", "tensor"),
        P(None, ("tensor", "dp"), None),
        P(None, "dp", "tensor"),
        P(None, ("tensor", "dp")),
        P(None, ("tensor", "dp"), None),
        P(None, ("dp", "tensor")),
        P(("dp", "tensor"), None),
    )
    return jax.shard_map(
        local,
        mesh=mesh,
        in_specs=placed,
        out_specs=(
            P(("dp", "tensor"), None),
            P(("dp", "tensor"), None),
            P(None, ("dp", "tensor")),
            P(None, ("dp", "tensor")),
            P(None, None, "dp", "tensor"),
            P(None, ("tensor", "dp"), None),
            P(None, "dp", "tensor"),
            P(None, ("tensor", "dp")),
            P(None, ("tensor", "dp"), None),
            P(None, ("dp", "tensor")),
        ),
        check_vma=False,
    )
```

profile of v0, /device:TPU:0, one launch (start us, length us, event | category | flops | bytes accessed | tf_op | source)
XLA Modules:
  0.0 2761.6 jit_solution(7765708808695252846)
XLA Ops:
  8.8 178.3 %all-gather.10 = bf16[128,8,2]{1,2,0:T(2,128)(2,1)S(1)} all-gather(bf16[1,8,2]{1,2,0:T(2,128)(2,1)} %bitcast.335), channel_id=1, replica_groups=mesh['dp'=32,'tensor'=4] {'dp','tensor'}, dimensions={0}, use_global_device_ids=true | all-gather | bytes 4128 | tf_op jit(solution)/shard_map/all_gather | solution.py:214
  187.2 169.8 %all-gather.11 = bf16[128,8,2]{1,2,0:T(2,128)(2,1)S(1)} all-gather(bf16[1,8,2]{1,2,0:T(2,128)(2,1)} %bitcast.336), channel_id=1, replica_groups=mesh['dp'=32,'tensor'=4] {'dp','tensor'}, dimensions={0}, use_global_device_ids=true | all-gather | bytes 4128 | tf_op jit(solution)/shard_map/all_gather | solution.py:215
  367.4 77.1 %all-reduce.15 = (bf16[1024]{0:T(1024)(128)(2,1)S(1)}, bf16[1024]{0:T(1024)(128)(2,1)S(1)}) all-reduce(bf16[1024]{0:T(1024)(128)(2,1)S(1)} %dynamic-update-slice.20, bf16[1024]{0:T(1024)(128)(2,1)S(1)} %dynamic-update-slice.21), channel_id=5, replica_groups=mesh['dp'=32,'tensor'=4] {'dp'}, use_global_device_ids=true, to_apply=%add.4 | all-reduce | flops 2048 | bytes 8192
  445.3 80.9 %all-gather.1 = bf16[1,256,1024]{2,1,0:T(8,128)(2,1)S(1)} all-gather(bf16[1,8,1024]{2,1,0:T(8,128)(2,1)S(1)} %get-tuple-element.220), channel_id=3, replica_groups=mesh['dp'=32,'tensor'=4] {'dp'}, dimensions={1}, use_global_device_ids=true | all-gather | bytes 540672 | tf_op jit(solution)/shard_map/all_gather | solution.py:229
  527.4 4.0 fusion.200
  541.0 6.6 fusion.58
  547.6 148.3 %all-gather.36.cloned.1.call-done = bf16[1,1024,1024]{2,1,0:T(8,128)(2,1)} async-done(((bf16[1,32,1024]{2,1,0:T(8,128)(2,1)}), bf16[1,1024,1024]{2,1,0:T(8,128)(2,1)}) %all-gather.36.cloned.1.call-update) | async-done | bytes 2097168 | tf_op jit(solution)/shard_map/all_gather | solution.py:232
  695.9 5.6 fusion.52
  701.5 2.8 convolution_add_fusion.1
  705.8 176.2 %all-gather.12 = bf16[128,8,2]{1,2,0:T(2,128)(2,1)S(1)} all-gather(bf16[1,8,2]{1,2,0:T(2,128)(2,1)S(1)} %bitcast.337), channel_id=1, replica_groups=mesh['dp'=32,'tensor'=4] {'dp','tensor'}, dimensions={0}, use_global_device_ids=true | all-gather | bytes 4128 | tf_op jit(solution)/shard_map/all_gather | solution.py:216
  887.7 79.0 %all-gather.6 = bf16[1,256,1024]{2,1,0:T(8,128)(2,1)S(1)} all-gather(bf16[1,8,1024]{2,1,0:T(8,128)(2,1)S(1)} %get-tuple-element.219), channel_id=8, replica_groups=mesh['dp'=32,'tensor'=4] {'dp'}, dimensions={1}, use_global_device_ids=true | all-gather | bytes 540672 | tf_op jit(solution)/shard_map/all_gather | solution.py:229
  969.3 3.9 fusion.205
  979.5 3.9 multiply_reduce_fusion.3
  990.1 4.8 multiply_convert_fusion.3
  1005.7 115.8 %all-gather.40.cloned.1.call-done = bf16[1,1024,1024]{2,1,0:T(8,128)(2,1)} async-done(((bf16[1,32,1024]{2,1,0:T(8,128)(2,1)}), bf16[1,1024,1024]{2,1,0:T(8,128)(2,1)}) %all-gather.40.cloned.1.call-update) | async-done | bytes 2097168 | tf_op jit(solution)/shard_map/all_gather | solution.py:230
  1121.5 6.6 fusion.44
  1128.1 149.0 %all-gather.42.cloned.1.call-done = bf16[1,1024,1024]{2,1,0:T(8,128)(2,1)} async-done(((bf16[1,32,1024]{2,1,0:T(8,128)(2,1)}), bf16[1,1024,1024]{2,1,0:T(8,128)(2,1)}) %all-gather.42.cloned.1.call-update) | async-done | bytes 2097168 | tf_op jit(solution)/shard_map/all_gather | solution.py:232
  1277.2 9.0 fusion.206
  1288.8 3.2 fusion.23
  1292.5 3.2 fusion.135
  1296.5 2.8 fusion.38
  1302.2 2.8 convolution_add_fusion
  1305.1 25.6 reduce-scatter.18.cloned.1.call-done
  1334.0 50.1 %reduce-scatter.16.cloned.1.call-done = f32[256,1024]{1,0:T(8,128)} async-done(((f32[1024,1024]{1,0:T(8,128)}), f32[256,1024]{1,0:T(8,128)}) %reduce-scatter.16.cloned.1.call-update) | async-done | bytes 1048592 | tf_op jit(solution)/shard_map/reduce_scatter | solution.py:148
  1384.1 3.4 fusion.184
  1390.8 5.0 fusion.85
  1395.8 4.2 copy.120
  1400.0 3.1 convolution_convert_fusion.4
  1403.3 12.2 all-gather.30.cloned.1.call-done
  1418.1 3.1 fusion.126
  1438.5 3.3 convolution_convert_fusion.5
  1441.9 3.7 fusion.130
  1447.6 3.6 fusion.88
  1454.1 8.4 fusion.207
  1465.0 3.2 fusion.22
  1468.3 7.3 convolution_convert_fusion
  1475.8 7.2 convolution_convert_fusion.1
  1483.1 5.9 convolution_convert_fusion.2
  1489.3 6.1 convolution_convert_fusion.3
  1496.1 82.0 %all-reduce.14 = (bf16[1024]{0:T(1024)(128)(2,1)S(1)}, bf16[1024]{0:T(1024)(128)(2,1)S(1)}) all-reduce(bf16[1024]{0:T(1024)(128)(2,1)S(1)} %copy-done.79, bf16[1024]{0:T(1024)(128)(2,1)S(1)} %get-tuple-element.258), channel_id=25, replica_groups=mesh['dp'=32,'tensor'=4] {'dp'}, use_global_device_ids=true, to_apply=%region_41.42.clone | all-reduce | flops 2048 | bytes 8192
  1578.9 157.1 %reduce-scatter.22.cloned.1.call-done = bf16[8,1024]{1,0:T(8,128)(2,1)} async-done(((bf16[256,1024]{1,0:T(8,128)(2,1)}), bf16[8,1024]{1,0:T(8,128)(2,1)}) %reduce-scatter.22.cloned.1.call-update) | async-done | bytes 16400 | tf_op jit(solution)/shard_map/reduce_scatter | solution.py:258
  1737.4 320.1 %all-reduce.19.cloned.1.call-done = (bf16[3,1024,256]{2,0,1:T(4,128)(2,1)}, bf16[3,1024,256]{2,0,1:T(4,128)(2,1)}) async-done(((bf16[3,1024,256]{2,0,1:T(4,128)(2,1)}, bf16[3,1024,256]{2,0,1:T(4,128)(2,1)}), (bf16[3,1024,256]{2,0,1:T(4,128)(2,1)}, bf16[3,1024,256]{2,0,1:T(4,128)(2,1)})) %all-reduce.19.cloned.1.call-update) | async-done | bytes 3145744
  2059.9 39.1 %reduce-scatter.20.cloned.1.call-done = bf16[256,1024]{1,0:T(8,128)(2,1)} async-done(((bf16[1024,1024]{1,0:T(8,128)(2,1)}), bf16[256,1024]{1,0:T(8,128)(2,1)}) %reduce-scatter.20.cloned.1.call-update) | async-done | bytes 524304 | tf_op jit(solution)/shard_map/reduce_scatter | solution.py:181
  2100.7 66.5 %all-reduce.13 = (f32[2,1024]{1,0:T(2,128)S(1)}, f32[2,1024]{1,0:T(2,128)S(1)}, f32[2,1024]{1,0:T(2,128)S(1)}) all-reduce(f32[2,1024]{1,0:T(2,128)S(1)} %pad_maximum_fusion.28, f32[2,1024]{1,0:T(2,128)S(1)} %pad_maximum_fusion.29, f32[2,1024]{1,0:T(2,128)S(1)} %pad_maximum_fusion.30), channel_id=16, replica_groups=mesh['dp'=32,'tensor'=4] {'dp','tensor'}, use_global_device_ids=true, to_apply=%region_28.29.clone | all-reduce | flops 6144 | bytes 49152
  2169.2 94.9 %reduce-scatter.32.cloned.1.call-done = bf16[32,1024]{1,0:T(8,128)(2,1)} async-done(((bf16[1024,1024]{1,0:T(8,128)(2,1)}), bf16[32,1024]{1,0:T(8,128)(2,1)}) %reduce-scatter.32.cloned.1.call-update) | async-done | bytes 65552 | tf_op jit(solution)/shard_map/reduce_scatter | solution.py:267
  2264.0 162.2 %reduce-scatter.30.cloned.1.call-done = bf16[32,1024]{1,0:T(8,128)(2,1)} async-done(((bf16[1024,1024]{1,0:T(8,128)(2,1)}), bf16[32,1024]{1,0:T(8,128)(2,1)}) %reduce-scatter.30.cloned.1.call-update) | async-done | bytes 65552 | tf_op jit(solution)/shard_map/reduce_scatter | solution.py:267
  2427.8 160.4 %reduce-scatter.28.cloned.1.call-done = bf16[32,1024]{1,0:T(8,128)(2,1)} async-done(((bf16[1024,1024]{1,0:T(8,128)(2,1)}), bf16[32,1024]{1,0:T(8,128)(2,1)}) %reduce-scatter.28.cloned.1.call-update) | async-done | bytes 65552 | tf_op jit(solution)/shard_map/reduce_scatter | solution.py:261
  2588.2 162.0 %reduce-scatter.26.cloned.1.call-done = bf16[32,1024]{1,0:T(8,128)(2,1)} async-done(((bf16[1024,1024]{1,0:T(8,128)(2,1)}), bf16[32,1024]{1,0:T(8,128)(2,1)}) %reduce-scatter.26.cloned.1.call-update) | async-done | bytes 65552 | tf_op jit(solution)/shard_map/reduce_scatter | solution.py:261
  (382 shorter events, 110.4 us)
Async XLA Ops:
  7.2 358.5 %copy-start.78 = (u32[128]{0:T(128)S(1)}, u32[128]{0:T(128)}, u32[]{:S(2)}) copy-start(u32[128]{0:T(128)} %constant.277) | copy-start | bytes 1540
  7.2 358.4 %copy-start.49 = (s32[1024]{0:T(1024)S(1)}, s32[1024]{0:T(1024)}, u32[]{:S(2)}) copy-start(s32[1024]{0:T(1024)} %param.36) | copy-start | bytes 12292
  7.2 358.5 %copy-start.80 = (bf16[2,32]{1,0:T(2,128)(2,1)S(1)}, bf16[2,32]{1,0:T(2,128)(2,1)}, u32[]{:S(2)}) copy-start(bf16[2,32]{1,0:T(2,128)(2,1)} %param.42) | copy-start | bytes 388
  7.2 438.0 %copy-start.57 = (bf16[2,8,1024]{2,1,0:T(8,128)(2,1)S(1)}, bf16[2,8,1024]{2,1,0:T(8,128)(2,1)}, u32[]{:S(2)}) copy-start(bf16[2,8,1024]{2,1,0:T(8,128)(2,1)} %param.40) | copy-start | bytes 98308
  7.2 520.1 %all-gather.32.cloned.1.call-start = ((), (), s32[]{:S(2)}) async-start(), calls=%async_computation.24 | async-start | bytes 1622016 | tf_op jit(solution)/shard_map/all_gather | solution.py:228
  8.8 518.6 %all-gather.24.cloned.1.call-start = ((), (), s32[]{:S(2)}) async-start(), calls=%async_computation.10 | async-start | bytes 2621440 | tf_op jit(solution)/shard_map/all_gather | solution.py:132
  358.8 85.8 %copy-start.65 = (f32[256]{0:T(256)}, f32[256]{0:T(256)S(1)}, u32[]{:S(2)}) copy-start(f32[256]{0:T(256)S(1)} %broadcast_multiply_fusion.5) | copy-start | bytes 3076
  360.1 85.1 %copy-start.69 = (f32[256]{0:T(256)}, f32[256]{0:T(256)S(1)}, u32[]{:S(2)}) copy-start(f32[256]{0:T(256)S(1)} %add_rsqrt_fusion.1) | copy-start | bytes 3076
  360.2 171.3 %copy-start.47 = (f32[1,1024]{1,0:T(1,128)}, f32[1,1024]{1,0:T(1,128)S(1)}, u32[]{:S(2)}) copy-start(f32[1,1024]{1,0:T(1,128)S(1)} %get-tuple-element.224) | copy-start | bytes 12292
  362.3 178.7 %all-gather.34.cloned.1.call-start = ((), (), s32[]{:S(2)}) async-start(), calls=%async_computation.25 | async-start | bytes 2162688 | tf_op jit(solution)/shard_map/all_gather | solution.py:230
  363.9 331.9 %all-gather.36.cloned.1.call-start = ((), (), s32[]{:S(2)}) async-start(), calls=%async_computation.26 | async-start | bytes 2162688 | tf_op jit(solution)/shard_map/all_gather | solution.py:232
  365.5 517.4 %reduce-scatter.14.cloned.1.call-start = ((), (), s32[]{:S(2)}) async-start(), calls=%async_computation.11 | async-start | bytes 5242880 | tf_op jit(solution)/shard_map/reduce_scatter | solution.py:148
  444.5 251.3 %copy-start.74 = (f32[1024]{0:T(1024)}, f32[1024]{0:T(1024)S(1)}, u32[]{:S(2)}) copy-start(f32[1024]{0:T(1024)S(1)} %convert_element_type.220) | copy-start | bytes 12292
  538.7 162.8 %copy-start.41 = (bf16[4,64,512]{2,1,0:T(8,128)(2,1)}, bf16[4,64,512]{2,1,0:T(8,128)(2,1)S(1)}, u32[]{:S(2)}) copy-start(bf16[4,64,512]{2,1,0:T(8,128)(2,1)S(1)} %fusion.136) | copy-start | bytes 786436
  540.9 160.6 %copy-start.42 = (bf16[4,64,512]{2,1,0:T(8,128)(2,1)}, bf16[4,64,512]{2,1,0:T(8,128)(2,1)S(1)}, u32[]{:S(2)}) copy-start(bf16[4,64,512]{2,1,0:T(8,128)(2,1)S(1)} %fusion.138) | copy-start | bytes 786436
  704.3 178.5 %copy-start.7 = (bf16[256,1024]{1,0:T(8,128)(2,1)S(1)}, bf16[256,1024]{1,0:T(8,128)(2,1)}, u32[]{:S(2)}) copy-start(bf16[256,1024]{1,0:T(8,128)(2,1)} %param.35) | copy-start | bytes 1572868
  704.4 262.3 %all-gather.28.cloned.1.call-start = ((), (), s32[]{:S(2)}) async-start(), calls=%async_computation.14 | async-start | bytes 2621440 | tf_op jit(solution)/shard_map/all_gather | solution.py:159
  705.0 264.3 %all-gather.38.cloned.1.call-start = ((), (), s32[]{:S(2)}) async-start(), calls=%async_computation.27 | async-start | bytes 1622016 | tf_op jit(solution)/shard_map/all_gather | solution.py:228
  705.7 263.6 %all-gather.26.cloned.1.call-start = ((), (), s32[]{:S(2)}) async-start(), calls=%async_computation.12 | async-start | bytes 2621440 | tf_op jit(solution)/shard_map/all_gather | solution.py:132
  884.6 84.6 %copy-start.73 = (f32[256]{0:T(256)}, f32[256]{0:T(256)S(1)}, u32[]{:S(2)}) copy-start(f32[256]{0:T(256)S(1)} %add_rsqrt_fusion) | copy-start | bytes 3076
  885.7 235.8 %all-gather.40.cloned.1.call-start = ((), (), s32[]{:S(2)}) async-start(), calls=%async_computation.28 | async-start | bytes 2162688 | tf_op jit(solution)/shard_map/all_gather | solution.py:230
  886.4 390.7 %all-gather.42.cloned.1.call-start = ((), (), s32[]{:S(2)}) async-start(), calls=%async_computation.29 | async-start | bytes 2162688 | tf_op jit(solution)/shard_map/all_gather | solution.py:232
  887.0 443.7 %reduce-scatter.18.cloned.1.call-start = ((), (), s32[]{:S(2)}) async-start(), calls=%async_computation.15 | async-start | bytes 2621440 | tf_op jit(solution)/shard_map/reduce_scatter | solution.py:181
  978.0 7.6 copy-start.1
  1005.7 271.5 %copy-start.76 = (f32[1024]{0:T(1024)S(1)}, f32[1024]{0:T(1024)}, u32[]{:S(2)}) copy-start(f32[1024]{0:T(1024)} %convert_element_type.221) | copy-start | bytes 12292
  1277.2 9.0 copy-start.84
  1292.0 92.1 %reduce-scatter.16.cloned.1.call-start = ((), (), s32[]{:S(2)}) async-start(), calls=%async_computation.13 | async-start | bytes 5242880 | tf_op jit(solution)/shard_map/reduce_scatter | solution.py:148
  1305.1 79.0 %copy-start.20 = (bf16[256,1024]{1,0:T(8,128)(2,1)S(1)}, bf16[256,1024]{1,0:T(8,128)(2,1)}, u32[]{:S(2)}) copy-start(bf16[256,1024]{1,0:T(8,128)(2,1)} %param.45) | copy-start | bytes 1572868
  1305.1 84.3 %copy-start.51 = (f32[4,512]{1,0:T(4,128)S(1)}, f32[4,512]{1,0:T(4,128)}, u32[]{:S(2)}) copy-start(f32[4,512]{1,0:T(4,128)} %copy-done.50) | copy-start | bytes 24580
  1305.1 110.4 %all-gather.30.cloned.1.call-start = ((), (), s32[]{:S(2)}) async-start(), calls=%async_computation.16 | async-start | bytes 2621440 | tf_op jit(solution)/shard_map/all_gather | solution.py:159
  1389.3 189.6 %reduce-scatter.24.cloned.1.call-start = ((), (), s32[]{:S(2)}) async-start(), calls=%async_computation.19 | async-start | bytes 540672 | tf_op jit(solution)/shard_map/reduce_scatter | solution.py:258
  1390.8 9.1 copy-start.44
  1403.1 332.9 %reduce-scatter.22.cloned.1.call-start = ((), (), s32[]{:S(2)}) async-start(), calls=%async_computation.18 | async-start | bytes 540672 | tf_op jit(solution)/shard_map/reduce_scatter | solution.py:258
  1438.5 7.2 copy-start.11
  1445.7 611.8 %all-reduce.19.cloned.1.call-start = ((), (), s32[]{:S(2)}) async-start(), calls=%async_computation.30 | async-start | bytes 8388608
  1453.9 645.2 %reduce-scatter.20.cloned.1.call-start = ((), (), s32[]{:S(2)}) async-start(), calls=%async_computation.17 | async-start | bytes 2621440 | tf_op jit(solution)/shard_map/reduce_scatter | solution.py:181
  1454.1 8.4 copy-start.82
  1468.2 795.8 %reduce-scatter.32.cloned.1.call-start = ((), (), s32[]{:S(2)}) async-start(), calls=%async_computation.23 | async-start | bytes 2162688 | tf_op jit(solution)/shard_map/reduce_scatter | solution.py:267
  1475.5 950.7 %reduce-scatter.30.cloned.1.call-start = ((), (), s32[]{:S(2)}) async-start(), calls=%async_computation.22 | async-start | bytes 2162688 | tf_op jit(solution)/shard_map/reduce_scatter | solution.py:267
  1483.1 1105.1 %reduce-scatter.28.cloned.1.call-start = ((), (), s32[]{:S(2)}) async-start(), calls=%async_computation.21 | async-start | bytes 2162688 | tf_op jit(solution)/shard_map/reduce_scatter | solution.py:261
  1489.1 609.9 %copy-start.8 = (bf16[256,1024]{1,0:T(8,128)(2,1)S(1)}, bf16[256,1024]{1,0:T(8,128)(2,1)}, u32[]{:S(2)}) copy-start(bf16[256,1024]{1,0:T(8,128)(2,1)} %param.35) | copy-start | bytes 1572868
  1489.2 609.9 %copy-start.48 = (f32[1,1024]{1,0:T(1,128)S(1)}, f32[1,1024]{1,0:T(1,128)}, u32[]{:S(2)}) copy-start(f32[1,1024]{1,0:T(1,128)} %copy-done.47) | copy-start | bytes 12292
  1489.2 609.9 %copy-start.66 = (f32[256]{0:T(256)S(1)}, f32[256]{0:T(256)}, u32[]{:S(2)}) copy-start(f32[256]{0:T(256)} %copy-done.65) | copy-start | bytes 3076
  1489.2 609.9 %copy-start.70 = (f32[256]{0:T(256)S(1)}, f32[256]{0:T(256)}, u32[]{:S(2)}) copy-start(f32[256]{0:T(256)} %copy-done.69) | copy-start | bytes 3076
  1489.2 611.5 %copy-start.68 = (f32[1024]{0:T(1024)S(1)}, f32[1024]{0:T(1024)}, u32[]{:S(2)}) copy-start(f32[1024]{0:T(1024)} %get-tuple-element.158) | copy-start | bytes 12292
  1489.2 611.5 %copy-start.67 = (f32[1024]{0:T(1024)S(1)}, f32[1024]{0:T(1024)}, u32[]{:S(2)}) copy-start(f32[1024]{0:T(1024)} %get-tuple-element.165) | copy-start | bytes 12292
  1489.2 1261.1 %reduce-scatter.26.cloned.1.call-start = ((), (), s32[]{:S(2)}) async-start(), calls=%async_computation.20 | async-start | bytes 2162688 | tf_op jit(solution)/shard_map/reduce_scatter | solution.py:261
  1495.3 1256.5 %copy-start.10 = (f32[256,1024]{1,0:T(8,128)S(1)}, f32[256,1024]{1,0:T(8,128)}, u32[]{:S(2)}) copy-start(f32[256,1024]{1,0:T(8,128)} %copy-done.9) | copy-start | bytes 3145732
  (67 other events, 226.6 us)
Sparse Core Ops, SparseCore 0:
  9.7 154.8 all-gather.31
  362.4 23.0 all-gather.23
  387.8 152.8 all-gather.33
  542.7 153.0 all-gather.35
  704.5 51.7 reduce-scatter.13
  757.9 26.0 all-gather.27
  785.8 151.8 all-gather.37
  940.1 27.0 all-gather.25
  968.9 152.5 all-gather.39
  1123.6 153.4 all-gather.41
  1292.1 38.5 reduce-scatter.17
  1333.2 50.8 reduce-scatter.15
  1389.4 26.0 all-gather.29
  1417.8 159.6 reduce-scatter.23
  1579.7 156.2 reduce-scatter.21
  1738.6 318.8 all-reduce.18
  2060.1 38.8 reduce-scatter.19
  2101.2 162.7 reduce-scatter.31
  2266.5 159.6 reduce-scatter.29
  2428.5 159.7 reduce-scatter.27
  2590.7 159.4 reduce-scatter.25
where the time goes:
time: 2770 us; the launch traced here: 2760 us
  waiting for transfers between devices  1600 us (58%)
  blocking collectives  910 us (33%)
  matrix products  154 us (6%)
  other arithmetic  44.4 us (2%)
  local copies, waits for them, and re-layouts  34.4 us (1%)
    unnamed x22, waiting for transfers between devices  323 us
    reduce_scatter x2, waiting for transfers between devices, local(): lax.psum_scatter(terms[2].astype(jnp.bfloat16), 'dp', scatter_dimension=0...  322 us
    all_gather x2, waiting for transfers between devices, local(): lax.all_gather(down_weight[layer], 'dp', axis=0, tiled=True)  297 us
    reduce_scatter x2, waiting for transfers between devices, local(): lax.psum_scatter(terms[4].astype(jnp.bfloat16), 'dp', scatter_dimension=0...  257 us
    unnamed x3, blocking collectives  226 us
    all_gather x1, blocking collectives, local(): lax.all_gather(norm_gain, ('dp', 'tensor'), axis=1, tiled=True)  178 us
    all_gather x1, blocking collectives, local(): lax.all_gather(final_bias, ('dp', 'tensor'), axis=1, tiled=True)  176 us
    all_gather x1, blocking collectives, local(): lax.all_gather(norm_shift, ('dp', 'tensor'), axis=1, tiled=True)  170 us
  transfers between devices with their start and end apart: 21, of which 13 were waited for; matrix products, arithmetic and copies ran while one was open for 7% of the time, Pallas kernels for 0%

commit v1 on v0

--- a/solution.py
+++ b/solution.py
@@ -1,16 +1,512 @@
+import functools
 import math
 
 import jax
 import jax.numpy as jnp
 from jax import lax
+from jax.experimental import pallas as pl
+from jax.experimental.pallas import tpu as pltpu
 from jax.sharding import PartitionSpec as P
 
 HEAD_DIM = 64
 ROT = 32
+MESH = pl.DeviceIdType.MESH
+ALL = slice(None)
 
 
 epsilon = 1e-05
 block_rows = 512
+
+
+class Place:
+    def __init__(self):
+        dp = lax.axis_index("dp")
+        self.t = lax.axis_index("tensor")
+        self.dp = dp
+        self.at = {"y": dp // 16, "x": lax.rem(dp // 4, 4), "z": lax.rem(dp, 4)}
+
+    def plus(self, axis, step):
+        return lax.rem(self.at[axis] + (step % 4), 4)
+
+    def peer(self, axis, step):
+        if axis == "core":
+            return (self.dp, self.t ^ 1)
+        if axis == "far":
+            return (self.dp, self.t ^ 2)
+        if axis == "both":
+            return (self.dp, self.t ^ 3)
+        c = dict(self.at)
+        c[axis] = 1 - c["y"] if axis == "y" else self.plus(axis, step)
+        return ((c["y"] * 4 + c["x"]) * 4 + c["z"], self.t)
+
+
+def meet(peers):
+    barrier = pltpu.get_barrier_semaphore()
+    for peer in peers:
+        pl.semaphore_signal(barrier, inc=1, device_id=peer, device_id_type=MESH)
+    pl.semaphore_wait(barrier, len(peers))
+
+
+def ring_peers(place):
+    return [place.peer(a, s) for a, s in (("x", 1), ("x", -1), ("z", 1), ("z", -1), ("y", 1))]
+
+
+def tensor_peers(place):
+    return [place.peer(a, 0) for a in ("core", "far", "both")]
+
+
+class Sems:
+    def __init__(self, send, recv):
+        self.send, self.recv, self.used = send, recv, 0
+
+    def take(self):
+        self.used += 1
+        return self.send.at[self.used - 1], self.recv.at[self.used - 1]
+
+
+class Link:
+    def __init__(self, sems, peer):
+        self.send, self.recv = sems.take()
+        self.peer = peer
+
+    def copy(self, src, dst):
+        return pltpu.make_async_remote_copy(
+            src_ref=src, dst_ref=dst, send_sem=self.send, recv_sem=self.recv,
+            device_id=self.peer, device_id_type=MESH,
+        )
+
+    def start(self, src, dst):
+        self.out = self.copy(src, dst)
+        self.out.start()
+
+    def arrived(self, dst):
+        self.copy(dst, dst).wait_recv()
+
+    def sent(self):
+        self.out.wait_send()
+
+
+def paths_of(columns, both):
+    half = columns // 2
+    if both:
+        return (("z", "x", pl.ds(0, half)), ("x", "z", pl.ds(half, half)))
+    return (("z", "x", pl.ds(0, columns)),)
+
+
+def region(ref, lead, where, cols):
+    return ref.at[(ALL,) * lead + (where["y"], where["x"], where["z"], ALL, cols)]
+
+
+class Gather:
+    links = 17
+    stages = 6
+
+    def __init__(self, place, sems, own, full, lead, local_sem):
+        self.place, self.own, self.full, self.lead, self.local_sem = place, own, full, lead, local_sem
+        self.paths = paths_of(full.shape[-1], full.shape[-1] % 256 == 0)
+        self.cross = Link(sems, place.peer("y", 1))
+        self.rings = []
+        for first, second, cols in self.paths:
+            self.rings.append(
+                [
+                    [Link(sems, place.peer(axis, 1)), Link(sems, place.peer(axis, -1)),
+                     Link(sems, place.peer(axis, 1)), Link(sems, place.peer(axis, -1))]
+                    for axis in (first, second)
+                ]
+            )
+
+    def _at(self, cols, **where):
+        return region(self.full, self.lead, where, cols)
+
+    def stage(self, number):
+        place, everything = self.place, pl.ds(0, self.full.shape[-1])
+        here = dict(place.at)
+        if number == 0:
+            mine = self._at(everything, **here)
+            self.local = pltpu.make_async_copy(self.own, mine, self.local_sem)
+            self.local.start()
+            self.cross.start(self.own, mine)
+            return
+        if number == 1:
+            self.local.wait()
+            self.cross.arrived(self._at(everything, **{**here, "y": 1 - here["y"]}))
+        for (first, second, cols), rings in zip(self.paths, self.rings):
+            axis = first if number <= 2 else second
+            other = here[second] if number <= 2 else ALL
+            rest = second if number <= 2 else first
+            ring = rings[0] if number <= 2 else rings[1]
+
+            def at(y, step):
+                index = here[axis] if step == 0 else place.plus(axis, step)
+                return self._at(cols, **{"y": y, axis: index, rest: other})
+
+            if number in (1, 3):
+                if number == 3:
+                    self._close(rings[0], first, second, cols, here[second])
+                ring[0].start(at(ALL, 0), at(ALL, 0))
+                ring[1].start(at(ALL, 0), at(ALL, 0))
+            elif number in (2, 4):
+                ring[0].arrived(at(ALL, -1))
+                ring[2].start(at(0, -1), at(0, -1))
+                ring[1].arrived(at(ALL, 1))
+                ring[3].start(at(1, 1), at(1, 1))
+            else:
+                self._close(ring, axis, rest, cols, ALL)
+        if number == 5:
+            self.cross.sent()
+            for rings in self.rings:
+                for ring in rings:
+                    for link in ring:
+                        link.sent()
+
+    def _close(self, ring, axis, rest, cols, other):
+        opposite = self.place.plus(axis, 2)
+        ring[2].arrived(self._at(cols, **{"y": 0, axis: opposite, rest: other}))
+        ring[3].arrived(self._at(cols, **{"y": 1, axis: opposite, rest: other}))
+
+
+class Reduce:
+    stages = 6
+
+    @staticmethod
+    def links(columns):
+        return 1 + 12 * len(paths_of(columns, columns % 256 == 0))
+
+    @staticmethod
+    def scratch(shape, dtype):
+        *lead, _, _, _, rows, columns = shape
+        lead = tuple(lead)
+        shapes = []
+        for _, _, cols in paths_of(columns, columns % 256 == 0):
+            w = cols.size
+            shapes += [pltpu.VMEM(lead + (2, 4, rows, w), dtype)]
+            shapes += [pltpu.VMEM(lead + (2, 2, 4, rows, w), dtype)]
+            shapes += [pltpu.VMEM(lead + (2, rows, w), dtype)]
+            shapes += [pltpu.VMEM(lead + (2, 2, rows, w), dtype)]
+        shapes += [pltpu.VMEM(lead + (2, rows, columns), jnp.float32)]
+        shapes += [pltpu.VMEM(lead + (rows, columns), dtype)] * 2
+        return shapes
+
+    def __init__(self, place, sems, given, total, lead, scratch):
+        self.place, self.given, self.total, self.lead = place, given, total, lead
+        columns = given.shape[-1]
+        self.dtype = given.dtype
+        self.paths = paths_of(columns, columns % 256 == 0)
+        self.cross = Link(sems, place.peer("y", 1))
+        self.work = []
+        for number, (first, second, cols) in enumerate(self.paths):
+            ends = []
+            for axis in (first, second):
+                ends.append([Link(sems, place.peer(axis, s)) for s in (1, -1, 1, -1, 1, -1)])
+            self.work.append((ends, scratch[4 * number : 4 * number + 4]))
+        self.summed, self.leaving, self.coming = scratch[-3:]
+
+    def _given(self, cols, **where):
+        return region(self.given, self.lead, where, cols)
+
+    def _pre(self, *index):
+        return (ALL,) * self.lead + index
+
+    def _add(self, into, *terms):
+        total = terms[0][...].astype(jnp.float32)
+        for term in terms[1:]:
+            total = total + term[...].astype(jnp.float32)
+        into[...] = total.astype(into.dtype)
+
+    def _send(self, links, near, far, at):
+        pre = self._pre
+        links[0].start(at(0, 2), near.at[pre(0)])
+        links[1].start(at(1, 2), near.at[pre(1)])
+        links[2].start(at(1, 1), far.at[pre(0, 1)])
+        links[3].start(at(0, -1), far.at[pre(1, 0)])
+
+    def _pass(self, links, near, far, at):
+        pre = self._pre
+        for way, step in ((0, 1), (1, -1)):
+            slot = near.at[pre(way)]
+            links[way].arrived(slot)
+            self._add(slot, slot, at(way, step))
+            links[4 + way].start(slot, far.at[pre(way, way)])
+
+    def _join(self, links, far):
+        pre = self._pre
+        links[2].arrived(far.at[pre(0, 1)])
+        links[3].arrived(far.at[pre(1, 0)])
+        links[4].arrived(far.at[pre(0, 0)])
+        links[5].arrived(far.at[pre(1, 1)])
+
+    def stage(self, number):
+        place, pre = self.place, self._pre
+        here = dict(place.at)
+        for (first, second, cols), (ends, (near1, far1, near2, far2)) in zip(self.paths, self.work):
+
+            def at1(y, step):
+                index = here[first] if step == 0 else place.plus(first, step)
+                return self._given(cols, **{"y": y, first: index, second: ALL})
+
+            def at2(y, step):
+                index = here[second] if step == 0 else place.plus(second, step)
+                return far1.at[pre(0, y, index)]
+
+            if number == 0:
+                self._send(ends[0], near1, far1, at1)
+            elif number == 1:
+                self._pass(ends[0], near1, far1, at1)
+            elif number == 2:
+                self._join(ends[0], far1)
+                for y in (0, 1):
+                    slot = far1.at[pre(0, y)]
+                    self._add(slot, slot, far1.at[pre(1, y)], at1(y, 0))
+                self._send(ends[1], near2, far2, at2)
+            elif number == 3:
+                self._pass(ends[1], near2, far2, at2)
+            elif number == 4:
+                self._join(ends[1], far2)
+                for y in (0, 1):
+                    into = self.summed.at[pre(y, ALL, cols)]
+                    self._add(into, at2(y, 0), far2.at[pre(0, y)], far2.at[pre(1, y)])
+        if number == 4:
+            self._add(self.leaving, self.summed.at[pre(1 - here["y"])])
+            self.cross.start(self.leaving, self.coming)
+        elif number == 5:
+            self.cross.arrived(self.coming)
+            self._add(self.total, self.summed.at[pre(here["y"])], self.coming)
+            self.cross.sent()
+            for ends, _ in self.work:
+                for links in ends:
+                    for link in links:
+                        link.sent()
+
+
+def skewed(jobs):
+    last = max(job.stages for job in jobs)
+    for step in range(len(jobs) + last):
+        for number in range(len(jobs) - 1, -1, -1):
+            stage = step - number
+            if 0 <= stage < jobs[number].stages:
+                jobs[number].stage(stage)
+
+
+def gather_kernel(shapes, *refs):
+    count = len(shapes)
+    small, owned = refs[0], refs[1 : 1 + count]
+    table, fulls = refs[1 + count], refs[2 + count : 2 + 2 * count]
+    four, tile, sends, recvs, locals_ = refs[2 + 2 * count :]
+    place = Place()
+    sems = Sems(sends, recvs)
+    meet(ring_peers(place) + tensor_peers(place))
+    links = [Link(sems, peer) for peer in tensor_peers(place)]
+    four[place.t] = small[...]
+    for link in links:
+        link.start(small, four.at[place.t])
+    jobs = [
+        Gather(place, sems, own, full, lead, locals_.at[number])
+        for number, (own, full, lead) in enumerate(zip(owned, fulls, shapes))
+    ]
+    for job in jobs:
+        job.stage(0)
+    for link, flip in zip(links, (1, 2, 3)):
+        link.arrived(four.at[place.t ^ flip])
+    row = lax.broadcasted_iota(jnp.int32, (8, 128), 0)
+    packed = jnp.zeros((8, 128), jnp.float32)
+    for t in range(4):
+        packed = jnp.where(row == t, four[t], packed)
+    tile[...] = packed
+    jobs = [Gather(place, sems, tile, table, 0, locals_.at[count])] + jobs
+    jobs[0].stage(0)
+    for job in jobs:
+        job.stages = 5
+        job.later = job.stage
+        job.stage = functools.partial(lambda stage, number: stage(number + 1), job.later)
+    skewed(jobs)
+    for link in links:
+        link.sent()
+
+
+def gather_weights(small, pieces):
+    outs = [jax.ShapeDtypeStruct((2, 4, 4, 8, 128), jnp.float32)]
+    for own, lead in pieces:
+        outs.append(jax.ShapeDtypeStruct(own.shape[:lead] + (2, 4, 4) + own.shape[lead:], own.dtype))
+    count = len(pieces)
+    number = 3 + Gather.links * (count + 1)
+    anywhere = pl.BlockSpec(memory_space=pl.ANY)
+    return pl.pallas_call(
+        functools.partial(gather_kernel, tuple(lead for _, lead in pieces)),
+        out_shape=outs,
+        in_specs=[pl.BlockSpec(memory_space=pltpu.VMEM)] + [anywhere] * count,
+        out_specs=[anywhere] * (count + 1),
+        scratch_shapes=[
+            pltpu.VMEM((4, 8, 128), jnp.float32),
+            pltpu.VMEM((8, 128), jnp.float32),
+            pltpu.SemaphoreType.DMA((number,)),
+            pltpu.SemaphoreType.DMA((number,)),
+            pltpu.SemaphoreType.DMA((count + 1,)),
+        ],
+        compiler_params=pltpu.CompilerParams(collective_id=0, has_side_effects=True),
+        name="gather_weights",
+    )(small, *[own for own, _ in pieces])
+
+
+def scatter_kernel(leads, *refs):
+    count = len(leads)
+    table, given = refs[0], refs[1 : 1 + count]
+    own_table, totals = refs[1 + count], refs[2 + count : 2 + 2 * count]
+    rest = list(refs[2 + 2 * count :])
+    four, tile, sends, recvs = rest[:4]
+    rest = rest[4:]
+    place = Place()
+    sems = Sems(sends, recvs)
+    meet(ring_peers(place) + tensor_peers(place))
+    jobs = []
+    for part, total, lead in zip((table,) + tuple(given), (tile,) + tuple(totals), (0,) + tuple(leads)):
+        need = 4 * len(paths_of(part.shape[-1], part.shape[-1] % 256 == 0)) + 3
+        jobs.append(Reduce(place, sems, part, total, lead, rest[:need]))
+        rest = rest[need:]
+    skewed(jobs)
+    links = [Link(sems, peer) for peer in tensor_peers(place)]
+    for number, link in enumerate(links):
+        link.start(tile, four.at[number])
+    whole = tile[...]
+    for number, link in enumerate(links):
+        link.arrived(four.at[number])
+        whole = whole + four[number]
+    own_table[...] = whole
+    for link in links:
+        link.sent()
+
+
+def scatter_grads(table, pieces):
+    outs = [jax.ShapeDtypeStruct((8, 128), jnp.float32)]
+    scratch = Reduce.scratch(table.shape, table.dtype)
+    number = 3 + Reduce.links(128)
+    for part, lead in pieces:
+        outs.append(jax.ShapeDtypeStruct(part.shape[:lead] + part.shape[lead + 3 :], jnp.float32))
+        scratch += Reduce.scratch(part.shape, part.dtype)
+        number += Reduce.links(part.shape[-1])
+    count = len(pieces)
+    inside = pl.BlockSpec(memory_space=pltpu.VMEM)
+    return pl.pallas_call(
+        functools.partial(scatter_kernel, tuple(lead for _, lead in pieces)),
+        out_shape=outs,
+        in_specs=[inside] * (count + 1),
+        out_specs=[inside] * (count + 1),
+        scratch_shapes=[
+            pltpu.VMEM((3, 8, 128), jnp.float32),
+            pltpu.VMEM((8, 128), jnp.float32),
+            pltpu.SemaphoreType.DMA((number,)),
+            pltpu.SemaphoreType.DMA((number,)),
+        ]
+        + scratch,
+        compiler_params=pltpu.CompilerParams(
+            collective_id=1, has_side_effects=True, vmem_limit_bytes=56 * 2**20
+        ),
+        name="scatter_grads",
+    )(table, *[part for part, _ in pieces])
+
+
+CHUNKS = 4
+
+
+def rows_kernel(own, full, local_sem, sends, recvs):
+    place = Place()
+    sems = Sems(sends, recvs)
+    t = place.t
+    meet([place.peer("core", 0), place.peer("far", 0)])
+    rows = own.shape[0] // CHUNKS
+    local = pltpu.make_async_copy(own, full.at[t], local_sem)
+    local.start()
+    far = [Link(sems, place.peer("far", 0)) for _ in range(CHUNKS)]
+    onward = [Link(sems, place.peer("core", 0)) for _ in range(CHUNKS)]
+    near = Link(sems, place.peer("core", 0))
+    part = [pl.ds(k * rows, rows) for k in range(CHUNKS)]
+    for k in range(CHUNKS):
+        far[k].start(own.at[part[k]], full.at[t, part[k]])
+    near.start(own, full.at[t])
+    for k in range(CHUNKS):
+        got = full.at[t ^ 2, part[k]]
+        far[k].arrived(got)
+        onward[k].start(got, got)
+    near.arrived(full.at[t ^ 1])
+    for k in range(CHUNKS):
+        onward[k].arrived(full.at[t ^ 3, part[k]])
+    for link in far + onward + [near]:
+        link.sent()
+    local.wait()
+
+
+def gather_rows(own):
+    count, width = own.shape
+    number = 2 * CHUNKS + 1
+    anywhere = pl.BlockSpec(memory_space=pl.ANY)
+    full = pl.pallas_call(
+        rows_kernel,
+        out_shape=jax.ShapeDtypeStruct((4, count, width), own.dtype),
+        in_specs=[anywhere],
+        out_specs=anywhere,
+        scratch_shapes=[
+            pltpu.SemaphoreType.DMA,
+            pltpu.SemaphoreType.DMA((number,)),
+            pltpu.SemaphoreType.DMA((number,)),
+        ],
+        compiler_params=pltpu.CompilerParams(collective_id=2, has_side_effects=True),
+        name="gather_rows",
+    )(own)
+    return full.reshape(4 * count, width)
+
+
+def sum_rows_kernel(given, total, pair, across, sends, recvs):
+    place = Place()
+    sems = Sems(sends, recvs)
+    t = place.t
+    meet([place.peer("core", 0), place.peer("far", 0)])
+    rows = given.shape[1] // CHUNKS
+    part = [pl.ds(k * rows, rows) for k in range(CHUNKS)]
+    to_core = [Link(sems, place.peer("core", 0)) for _ in range(CHUNKS)]
+    far = [Link(sems, place.peer("far", 0)) for _ in range(CHUNKS)]
+    near = Link(sems, place.peer("core", 0))
+    for k in range(CHUNKS):
+        to_core[k].start(given.at[t ^ 3, part[k]], pair.at[0, part[k]])
+    near.start(given.at[t ^ 1], pair.at[1])
+    for k in range(CHUNKS):
+        slot = pair.at[0, part[k]]
+        to_core[k].arrived(slot)
+        slot[...] = (
+            slot[...].astype(jnp.float32) + given[t ^ 2, part[k]].astype(jnp.float32)
+        ).astype(slot.dtype)
+        far[k].start(slot, across.at[part[k]])
+    near.arrived(pair.at[1])
+    for k in range(CHUNKS):
+        far[k].arrived(across.at[part[k]])
+        total[part[k]] = (
+            given[t, part[k]].astype(jnp.float32)
+            + pair[1, part[k]].astype(jnp.float32)
+            + across[part[k]].astype(jnp.float32)
+        )
+    for link in to_core + far + [near]:
+        link.sent()
+
+
+def sum_rows(partial):
+    count, width = partial.shape
+    number = 2 * CHUNKS + 1
+    inside = pl.BlockSpec(memory_space=pltpu.VMEM)
+    own = count // 4
+    return pl.pallas_call(
+        sum_rows_kernel,
+        out_shape=jax.ShapeDtypeStruct((own, width), jnp.float32),
+        in_specs=[inside],
+        out_specs=inside,
+        scratch_shapes=[
+            pltpu.VMEM((2, own, width), partial.dtype),
+            pltpu.VMEM((own, width), partial.dtype),
+            pltpu.SemaphoreType.DMA((number,)),
+            pltpu.SemaphoreType.DMA((number,)),
+        ],
+        compiler_params=pltpu.CompilerParams(
+            collective_id=3, has_side_effects=True, vmem_limit_bytes=32 * 2**20
+        ),
+        name="sum_rows",
+    )(partial.reshape(4, own, width))
 
 
 def seq_positions(segments):
@@ -129,7 +625,7 @@
     inverse = lax.rsqrt(jnp.mean(center * center, axis=-1, keepdims=True) + epsilon)
     unit = center * inverse
     normed_own = (unit * gain + shift).astype(jnp.bfloat16)
-    normed = lax.all_gather(normed_own, "tensor", axis=0, tiled=True)
+    normed = gather_rows(normed_own)
     count = normed.shape[0]
     joined = jnp.einsum("td,cde->cte", normed, qkv_full, preferred_element_type=jnp.float32)
     joined = joined.reshape(3, count, -1, HEAD_DIM)
@@ -138,14 +634,12 @@
     values = joined[2].astype(jnp.bfloat16)
     attended, logsum = attend_forward(query, keys, values, segments)
     attended = attended.astype(jnp.bfloat16).reshape(count, -1)
-    up = jnp.dot(normed, up_full, preferred_element_type=jnp.float32) + hidden_full.astype(
-        jnp.float32
-    )
+    up = jnp.dot(normed, up_full, preferred_element_type=jnp.float32) + hidden_full
     active = jax.nn.gelu(up, approximate=True).astype(jnp.bfloat16)
     local_sum = jnp.dot(attended, proj_full, preferred_element_type=jnp.float32) + jnp.dot(
         active, down_full, preferred_element_type=jnp.float32
     )
-    branch = lax.psum_scatter(local_sum, "tensor", scatter_dimension=0, tiled=True)
+    branch = sum_rows(local_sum.astype(jnp.bfloat16))
     result = state + branch + bias_final
     kept = (unit, inverse, normed, query, keys, values, logsum, attended, up, active)
     return (result, kept)
@@ -156,7 +650,7 @@
     unit, inverse, normed, query, keys, values, logsum, attended, up, active = kept
     count = normed.shape[0]
     grad_final = jnp.sum(grad, axis=0)
-    grad_rows = lax.all_gather(grad.astype(jnp.bfloat16), "tensor", axis=0, tiled=True)
+    grad_rows = gather_rows(grad.astype(jnp.bfloat16))
     grad_down = contract_rows(active, grad_rows)
     grad_active = contract_cols(grad_rows, down_full)
     _, gelu_back = jax.vjp(lambda value: jax.nn.gelu(value, approximate=True), up)
@@ -178,9 +672,7 @@
     grad_normed = grad_normed + jnp.einsum(
         "cte,cde->td", grad_joined, qkv_full, preferred_element_type=jnp.float32
     )
-    grad_own = lax.psum_scatter(
-        grad_normed.astype(jnp.bfloat16), "tensor", scatter_dimension=0, tiled=True
-    ).astype(jnp.float32)
+    grad_own = sum_rows(grad_normed.astype(jnp.bfloat16))
     grad_gain = jnp.sum(grad_own * unit, axis=0)
     grad_shift = jnp.sum(grad_own, axis=0)
     scaled = grad_own * gain
@@ -194,6 +686,14 @@
         (grad_qkv, grad_proj, grad_upw, grad_hidden, grad_down),
         (grad_gain, grad_shift, grad_final),
     )
+
+
+def fold(rows):
+    return jnp.concatenate([rows[..., :512], rows[..., 512:]], axis=-2)
+
+
+def unfold(rows):
+    return jnp.concatenate([rows[..., :8, :], rows[..., 8:, :]], axis=-1)
 
 
 def local(
@@ -210,87 +710,90 @@
     cotangent,
 ):
     layers = qkv_weight.shape[0]
-    gains, shifts, finals = (
-        lax.all_gather(norm_gain, ("dp", "tensor"), axis=1, tiled=True),
-        lax.all_gather(norm_shift, ("dp", "tensor"), axis=1, tiled=True),
-        lax.all_gather(final_bias, ("dp", "tensor"), axis=1, tiled=True),
-    )
-    gains = gains.astype(jnp.float32)
-    shifts = shifts.astype(jnp.float32)
-    finals = finals.astype(jnp.float32)
+    f32 = jnp.float32
+    row = jnp.concatenate(
+        [norm_gain.reshape(16), norm_shift.reshape(16), final_bias.reshape(16), hidden_bias.reshape(64)]
+    ).astype(f32)
+    small = jnp.broadcast_to(jnp.pad(row, (0, 16))[None], (8, 128))
+    pieces = []
+    proj_own = fold(proj_weight)
+    for layer in range(layers):
+        pieces += [
+            (qkv_weight[layer], 1), (up_weight[layer], 0), (down_weight[layer], 0), (proj_own[layer], 0)
+        ]
+    table, *wholes = gather_weights(small, pieces)
+    table = table.reshape(32, 8, 128)[:, :4]
+
+    def features(start):
+        return table[:, :, start : start + 16].reshape(128, 2, 8).transpose(1, 0, 2).reshape(2, 1024)
+
+    gains, shifts, finals = features(0), features(16), features(32)
+    t = lax.axis_index("tensor")
+    mine = lax.dynamic_index_in_dim(table, t, axis=1, keepdims=False)
+    hidden = mine[:, 48:112].reshape(32, 2, 32).transpose(1, 0, 2).reshape(2, 1024)
+    weights = []
+    for layer in range(layers):
+        qkv, up, down, proj = wholes[4 * layer : 4 * layer + 4]
+        weights.append(
+            (
+                qkv.reshape(3, 1024, 256),
+                unfold(proj.reshape(32, 16, 512)).reshape(256, 1024),
+                up.reshape(1024, 1024),
+                hidden[layer],
+                down.reshape(1024, 1024),
+            )
+        )
     positions = seq_positions(segment_ids)
     cosine, sine = rotary_tables(positions)
     state = tokens.astype(jnp.float32)
     saved = []
-    held = []
     for layer in range(layers):
-        weights = (
-            lax.all_gather(qkv_weight[layer], "dp", axis=1, tiled=True),
-            lax.all_gather(proj_weight[layer], "dp", axis=0, tiled=True),
-            lax.all_gather(up_weight[layer], "dp", axis=0, tiled=True),
-            lax.all_gather(hidden_bias[layer], "dp", axis=0, tiled=True),
-            lax.all_gather(down_weight[layer], "dp", axis=0, tiled=True),
-        )
         state, kept = layer_forward(
-            state, gains[layer], shifts[layer], weights, finals[layer], segment_ids, cosine, sine
+            state, gains[layer], shifts[layer], weights[layer], finals[layer], segment_ids, cosine, sine
         )
         saved.append(kept)
-        held.append(weights)
     mixed = state.astype(jnp.bfloat16)
     grad = cotangent.astype(jnp.float32)
     weight_terms = [None] * layers
     norm_terms = [None] * layers
     for layer in reversed(range(layers)):
-        weights = (
-            lax.all_gather(qkv_weight[layer], "dp", axis=1, tiled=True),
-            lax.all_gather(proj_weight[layer], "dp", axis=0, tiled=True),
-            lax.all_gather(up_weight[layer], "dp", axis=0, tiled=True),
-            lax.all_gather(hidden_bias[layer], "dp", axis=0, tiled=True),
-            lax.all_gather(down_weight[layer], "dp", axis=0, tiled=True),
-        )
-        grad, terms, small = layer_backward(
-            grad, gains[layer], weights, saved[layer], segment_ids, cosine, sine
-        )
-        weight_terms[layer] = (
-            lax.psum_scatter(
-                terms[0].astype(jnp.bfloat16), "dp", scatter_dimension=1, tiled=True
-            ).astype(jnp.float32),
-            lax.psum_scatter(
-                terms[1].astype(jnp.bfloat16), "dp", scatter_dimension=0, tiled=True
-            ).astype(jnp.float32),
-            lax.psum_scatter(
-                terms[2].astype(jnp.bfloat16), "dp", scatter_dimension=0, tiled=True
-            ).astype(jnp.float32),
-            lax.psum_scatter(
-                terms[3].astype(jnp.bfloat16), "dp", scatter_dimension=0, tiled=True
-            ).astype(jnp.float32),
-            lax.psum_scatter(
-                terms[4].astype(jnp.bfloat16), "dp", scatter_dimension=0, tiled=True
-            ).astype(jnp.float32),
-        )
-        norm_terms[layer] = small
-    stacked = tuple(
-        (jnp.stack([weight_terms[layer][member] for layer in range(layers)]) for member in range(5))
-    )
-    norm_stack = tuple(
-        (jnp.stack([norm_terms[layer][member] for layer in range(layers)]) for member in range(3))
-    )
-    grad_gain, grad_shift, grad_final = (
-        lax.psum_scatter(norm_stack[0], ("dp", "tensor"), scatter_dimension=1, tiled=True),
-        lax.psum_scatter(norm_stack[1], ("dp", "tensor"), scatter_dimension=1, tiled=True),
-        lax.psum_scatter(norm_stack[2], ("dp", "tensor"), scatter_dimension=1, tiled=True),
-    )
+        grad, weight_terms[layer], norm_terms[layer] = layer_backward(
+            grad, gains[layer], weights[layer], saved[layer], segment_ids, cosine, sine
+        )
+    low = jnp.bfloat16
+    parts = []
+    for layer in reversed(range(layers)):
+        qkv, proj, up, _, down = weight_terms[layer]
+        parts += [
+            (down.astype(low).reshape(2, 4, 4, 32, 1024), 0),
+            (up.astype(low).reshape(2, 4, 4, 32, 1024), 0),
+            (fold(proj.reshape(32, 8, 1024)).astype(low).reshape(2, 4, 4, 16, 512), 0),
+            (qkv.astype(low).reshape(3, 2, 4, 4, 32, 256), 1),
+        ]
+
+    def spread(member):
+        both = jnp.stack([norm_terms[layer][member] for layer in range(layers)])
+        return both.reshape(2, 32, 4, 8).transpose(1, 2, 0, 3).reshape(32, 4, 16)
+
+    hid = jnp.stack([weight_terms[layer][3] for layer in range(layers)])
+    hid = hid.reshape(2, 32, 32).transpose(1, 0, 2).reshape(32, 1, 64)
+    hid = jnp.where(jnp.arange(4)[None, :, None] == t, hid, 0.0)
+    sums = jnp.concatenate([spread(0), spread(1), spread(2), hid], axis=-1)
+    sums = jnp.pad(sums, ((0, 0), (0, 4), (0, 16))).reshape(2, 4, 4, 8, 128)
+    own_sums, *owned = scatter_grads(sums, parts)
+    line = lax.dynamic_index_in_dim(own_sums, t, axis=0, keepdims=False)
+    down, up, proj, qkv = [jnp.stack([owned[4 + k], owned[k]]) for k in range(4)]
     return (
         mixed,
         grad,
-        grad_gain,
-        grad_shift,
-        stacked[0],
-        stacked[1],
-        stacked[2],
-        stacked[3],
-        stacked[4],
-        grad_final,
+        line[0:16].reshape(2, 8),
+        line[16:32].reshape(2, 8),
+        qkv,
+        unfold(proj),
+        up,
+        line[48:112].reshape(2, 32),
+        down,
+        line[32:48].reshape(2, 8),
     )
 
 

time: 2770 us -> 551 us (0.20)
  waiting for transfers between devices: 1600 us -> 0 us
  blocking collectives: 910 us -> 0 us
  Pallas kernels: 0 us -> 325 us
  matrix products: 154 us -> 126 us
    reduce_scatter x10 -> x0, waiting for transfers between devices: 851 us -> none  [the longest x2 322 us: local(): lax.psum_scatter(terms[2].astype(jnp.bfloat16), 'dp', scatter_dimension=0...]
    all_gather x5 -> x0, blocking collectives: 684 us -> none  [the longest x1 178 us: local(): lax.all_gather(norm_gain, ('dp', 'tensor'), axis=1, tiled=True)]
    all_gather x10 -> x0, waiting for transfers between devices: 425 us -> none  [the longest x2 297 us: local(): lax.all_gather(down_weight[layer], 'dp', axis=0, tiled=True)]
    pallas_call x0 -> x10, Pallas kernels: none -> 325 us  [the longest x1 90.5 us: gather_weights(): pl.pallas_call(functools.partial(gather_kernel, tuple((lead for _, lead i...]
    unnamed x22 -> x0, waiting for transfers between devices: 323 us -> none
    unnamed x3 -> x0, blocking collectives: 226 us -> none
  transfers between devices with their start and end apart: 21 -> 0, of which waited for: 13 -> 0; matrix products, arithmetic and copies ran while one was open for 7% -> 0% of each run, Pallas kernels for 0% -> 0%
where the time goes in v1:
time: 551 us; the launch traced here: 541 us
  Pallas kernels  325 us (59%)
  matrix products  126 us (23%)
  local copies, waits for them, and re-layouts  46 us (8%)
  other arithmetic  40.4 us (7%)
    pallas_call x1, Pallas kernels, gather_weights(): pl.pallas_call(functools.partial(gather_kernel, tuple((lead for _, lead i...  90.5 us
    pallas_call x1, Pallas kernels, scatter_grads(): pl.pallas_call(functools.partial(scatter_kernel, tuple((lead for _, lead...  88.5 us
    pallas_call x4, Pallas kernels, gather_rows(): pl.pallas_call(rows_kernel, out_shape=jax.ShapeDtypeStruct((4, count, wid...  79.4 us
    pallas_call x4, Pallas kernels, sum_rows(): pl.pallas_call(sum_rows_kernel, out_shape=jax.ShapeDtypeStruct((own, widt...  66.3 us
    dot_general x6, matrix products, contract_cols(): lax.dot_general(left, right, (((1,), (1,)), ((), ())), preferred_element_...  24.4 us
    dot_general x6, matrix products, contract_rows(): lax.dot_general(left, right, (((0,), (0,)), ((), ())), preferred_element_...  23.5 us

profile of v1, /device:TPU:0, one launch (start us, length us, event | category | flops | bytes accessed | tf_op | source)
XLA Modules:
  0.0 540.6 jit_solution(12397938018566658045)
XLA Ops:
  16.8 2.1 fusion.41
  18.9 20.4 %gather_rows.6 = bf16[4,256,1024]{2,1,0:T(8,128)(2,1)} custom-call(bf16[256,1024]{1,0:T(8,128)(2,1)} %own), custom_call_target="tpu_custom_call" | custom-call | tf_op jit(solution)/shard_map/gather_rows/pallas_call | solution.py:441
  39.4 90.5 %gather_weights.1 = (f32[2,4,4,8,128]{4,3,2,1,0:T(8,128)}, bf16[3,2,4,4,32,256]{5,4,3,2,1,0:T(8,128)(2,1)}, bf16[2,4,4,32,1024]{4,3,2,1,0:T(8,128)(2,1)}, bf16[2...) custom-call(f32[8,128]{1,0:T(8,128)} %broadcast_in_dim.69.refs_0_, ...), custom_call_target="tpu_custom_call" | custom-call | tf_op jit(solution)/shard_map/gather_weights/pallas_call | solution.py:333
  141.2 20.3 %gather_rows.4 = bf16[4,256,1024]{2,1,0:T(8,128)(2,1)} custom-call(bf16[256,1024]{1,0:T(8,128)(2,1)} %fusion.92.own), custom_call_target="tpu_custom_call" | custom-call | tf_op jit(solution)/shard_map/gather_rows/pallas_call | solution.py:441
  161.6 4.7 fusion.161
  166.3 2.8 fusion.138
  169.9 2.2 fusion.155
  176.6 1.8 fusion.156
  178.4 1.9 fusion
  181.6 2.1 fusion.90
  184.6 16.0 %sum_rows.4 = f32[256,1024]{1,0:T(8,128)S(1)} custom-call(bf16[4,256,1024]{2,1,0:T(8,128)(2,1)S(1)} %bitcast.256), custom_call_target="tpu_custom_call" | custom-call | tf_op jit(solution)/shard_map/sum_rows/pallas_call | solution.py:494
  202.9 18.9 %gather_rows.5 = bf16[4,256,1024]{2,1,0:T(8,128)(2,1)} custom-call(bf16[256,1024]{1,0:T(8,128)(2,1)} %add_convert_fusion.3.own), custom_call_target="tpu_custom_call" | custom-call | tf_op jit(solution)/shard_map/gather_rows/pallas_call | solution.py:441
  221.8 4.7 fusion.162
  226.5 4.4 convolution_convert_fusion.3
  230.9 6.2 %convert_reduce_fusion = (f32[1024]{0:T(1024)S(1)}, bf16[1024,1024]{1,0:T(8,128)(2,1)}) fusion(f32[1024,1024]{1,0:T(8,128)S(1)} %fusion.162, f32[1024]{0:T(1024)S(1)} %copy-done.81, bf16[1024,1024]{1,0:T(8,128)(2,1)S(1)} %bitcast.356, bf16[1024,1024]{1,0:T(8,128)(2,1)S(1)} %bitcast.291), kind=kOutput, calls=%fused_computation.45 | convolution fusion | flops 2171599872 | bytes 10493952 | tf_op jit(solution)/shard_map/dot_general | solution.py:543
  237.2 4.7 fusion.139
  242.6 6.1 %convolution_convert_fusion.2 = bf16[1024,1024]{1,0:T(8,128)(2,1)} fusion(bf16[1024,1024]{1,0:T(8,128)(2,1)} %bitcast.294, bf16[1024,1024]{1,0:T(8,128)(2,1)} %get-tuple-element.280), kind=kOutput, calls=%fused_computation.81 | convolution fusion | flops 2148532224 | bytes 6291456 | tf_op jit(solution)/shard_map/dot_general | solution.py:537
  248.7 4.3 fusion.163
  253.1 1.8 fusion.160
  263.6 1.8 fusion.158
  265.4 1.7 fusion.1
  271.4 5.2 fusion.89
  278.9 16.3 %sum_rows.5 = f32[256,1024]{1,0:T(8,128)S(1)} custom-call(bf16[4,256,1024]{2,1,0:T(8,128)(2,1)S(1)} %bitcast.255), custom_call_target="tpu_custom_call" | custom-call | tf_op jit(solution)/shard_map/sum_rows/pallas_call | solution.py:494
  296.2 2.6 multiply_reduce_fusion.1
  298.8 2.2 multiply_convert_fusion.1
  305.6 5.1 fusion.23
  310.7 3.0 fusion.44
  313.8 2.6 copy.122
  316.4 17.2 %sum_rows.6 = f32[256,1024]{1,0:T(8,128)S(1)} custom-call(bf16[4,256,1024]{2,1,0:T(8,128)(2,1)S(1)} %bitcast.257), custom_call_target="tpu_custom_call" | custom-call | tf_op jit(solution)/shard_map/sum_rows/pallas_call | solution.py:494
  333.7 1.7 multiply_reduce_fusion.4
  340.4 19.8 %gather_rows.7 = bf16[4,256,1024]{2,1,0:T(8,128)(2,1)} custom-call(bf16[256,1024]{1,0:T(8,128)(2,1)} %convert_element_type.176.own), custom_call_target="tpu_custom_call" | custom-call | tf_op jit(solution)/shard_map/gather_rows/pallas_call | solution.py:441
  360.2 2.5 convolution_convert_fusion.8
  362.8 2.5 convolution_convert_fusion.6
  366.2 6.3 %convert_reduce_fusion.1 = (f32[1024]{0:T(1024)S(1)}, bf16[1024,1024]{1,0:T(8,128)(2,1)}) fusion(f32[1024,1024]{1,0:T(8,128)S(1)} %copy-done.91, f32[1024]{0:T(1024)S(1)} %copy-done.80, bf16[1024,1024]{1,0:T(8,128)(2,1)S(1)} %bitcast.299, bf16[1024,1024]{1,0:T(8,128)(2,1)S(1)} %bitcast.353), kind=kOutput, calls=%fused_computation.46 | convolution fusion | flops 2171599872 | bytes 10493952 | tf_op jit(solution)/shard_map/dot_general | solution.py:543
  372.5 4.4 convolution_convert_fusion.1
  377.9 3.0 fusion.78
  380.8 5.0 fusion.65
  386.9 5.4 %convolution_convert_fusion = bf16[1024,1024]{1,0:T(8,128)(2,1)} fusion(bf16[1024,1024]{1,0:T(8,128)(2,1)S(1)} %bitcast.287, bf16[1024,1024]{1,0:T(8,128)(2,1)} %get-tuple-element.196), kind=kOutput, calls=%fused_computation.79 | convolution fusion | flops 2148532224 | bytes 6291456 | tf_op jit(solution)/shard_map/dot_general | solution.py:537
  392.3 4.3 fusion.164
  401.7 2.8 multiply_reduce_fusion
  404.4 1.7 multiply_convert_fusion
  410.0 4.8 fusion.22
  414.8 3.0 fusion.45
  417.8 2.9 copy.124
  420.8 16.7 %sum_rows.7 = f32[256,1024]{1,0:T(8,128)S(1)} custom-call(bf16[4,256,1024]{2,1,0:T(8,128)(2,1)S(1)} %bitcast.258), custom_call_target="tpu_custom_call" | custom-call | tf_op jit(solution)/shard_map/sum_rows/pallas_call | solution.py:494
  441.1 88.5 %scatter_grads.1 = (f32[8,128]{1,0:T(8,128)}, f32[32,1024]{1,0:T(8,128)}, f32[32,1024]{1,0:T(8,128)}, f32[16,512]{1,0:T(8,128)}, f32[3,32,256]{2,1,0:T(8,128)}, ...) custom-call(f32[2,4,4,8,128]{4,3,2,1,0:T(8,128)} %bitcast.319, ...), custom_call_target="tpu_custom_call" | custom-call | tf_op jit(solution)/shard_map/scatter_grads/pallas_call | solution.py:388
  536.7 1.7 pad_maximum_fusion.26
  538.4 1.7 pad_maximum_fusion.27
  (359 shorter events, 85.1 us)
Async XLA Ops:
  5.0 131.9 %copy-start.6 = (bf16[256,1024]{1,0:T(8,128)(2,1)S(1)}, bf16[256,1024]{1,0:T(8,128)(2,1)}, u32[]{:S(2)}) copy-start(bf16[256,1024]{1,0:T(8,128)(2,1)} %param.35) | copy-start | bytes 1572868
  6.3 131.7 %copy-start.69 = (f32[256]{0:T(256)}, f32[256]{0:T(256)S(1)}, u32[]{:S(2)}) copy-start(f32[256]{0:T(256)S(1)} %broadcast_multiply_fusion.5) | copy-start | bytes 3076
  7.6 129.2 %copy-start.76 = (f32[256]{0:T(256)}, f32[256]{0:T(256)S(1)}, u32[]{:S(2)}) copy-start(f32[256]{0:T(256)S(1)} %add_rsqrt_fusion.1) | copy-start | bytes 3076
  15.9 156.4 %copy-start.42 = (f32[1024,16]{0,1:T(8,128)}, f32[1024,16]{0,1:T(8,128)S(1)}, u32[]{:S(2)}) copy-start(f32[1024,16]{0,1:T(8,128)S(1)} %get-tuple-element.255) | copy-start | bytes 196612
  39.4 101.0 %copy-start.19 = (bf16[4,256,1024]{2,1,0:T(8,128)(2,1)S(1)}, bf16[4,256,1024]{2,1,0:T(8,128)(2,1)}, u32[]{:S(2)}) copy-start(bf16[4,256,1024]{2,1,0:T(8,128)(2,1)} %gather_rows.6) | copy-start | bytes 6291460
  134.2 67.0 %copy-start.65 = (f32[1024]{0:T(1024)}, f32[1024]{0:T(1024)S(1)}, u32[]{:S(2)}) copy-start(f32[1024]{0:T(1024)S(1)} %mul.525) | copy-start | bytes 12292
  139.0 44.8 %copy-start.34 = (bf16[32,8,512]{2,1,0:T(8,128)(2,1)}, bf16[32,8,512]{2,1,0:T(8,128)(2,1)S(1)}, u32[]{:S(2)}) copy-start(bf16[32,8,512]{2,1,0:T(8,128)(2,1)S(1)} %get-tuple-element.231) | copy-start | bytes 786436
  139.1 44.8 %copy-start.36 = (bf16[32,8,512]{2,1,0:T(8,128)(2,1)}, bf16[32,8,512]{2,1,0:T(8,128)(2,1)S(1)}, u32[]{:S(2)}) copy-start(bf16[32,8,512]{2,1,0:T(8,128)(2,1)S(1)} %get-tuple-element.232) | copy-start | bytes 786436
  172.6 7.7 %copy-start.25 = (bf16[1,1024,256]{1,2,0:T(8,128)(2,1)}, bf16[1,1024,256]{1,2,0:T(8,128)(2,1)S(1)}, u32[]{:S(2)}) copy-start(bf16[1,1024,256]{1,2,0:T(8,128)(2,1)S(1)} %slice.623) | copy-start | bytes 1572868
  176.5 7.4 %copy-start.51 = (bf16[4,64,512]{2,1,0:T(8,128)(2,1)}, bf16[4,64,512]{2,1,0:T(8,128)(2,1)S(1)}, u32[]{:S(2)}) copy-start(bf16[4,64,512]{2,1,0:T(8,128)(2,1)S(1)} %fusion.88) | copy-start | bytes 786436
  183.8 16.9 %copy-start.53 = (bf16[4,64,512]{2,1,0:T(8,128)(2,1)}, bf16[4,64,512]{2,1,0:T(8,128)(2,1)S(1)}, u32[]{:S(2)}) copy-start(bf16[4,64,512]{2,1,0:T(8,128)(2,1)S(1)} %fusion.90) | copy-start | bytes 786436
  183.8 16.8 %copy-start.75 = (f32[1024]{0:T(1024)S(1)}, f32[1024]{0:T(1024)}, u32[]{:S(2)}) copy-start(f32[1024]{0:T(1024)} %add.269) | copy-start | bytes 12292
  200.9 25.6 %copy-start.71 = (f32[256]{0:T(256)}, f32[256]{0:T(256)S(1)}, u32[]{:S(2)}) copy-start(f32[256]{0:T(256)S(1)} %broadcast_multiply_fusion.4) | copy-start | bytes 3076
  201.8 24.6 %copy-start.73 = (f32[256]{0:T(256)}, f32[256]{0:T(256)S(1)}, u32[]{:S(2)}) copy-start(f32[256]{0:T(256)S(1)} %add_rsqrt_fusion) | copy-start | bytes 3076
  242.6 6.1 %copy-start.86 = (bf16[2,4,4,32,1024]{4,3,2,1,0:T(8,128)(2,1)S(1)}, bf16[2,4,4,32,1024]{4,3,2,1,0:T(8,128)(2,1)}, u32[]{:S(2)}) copy-start(bf16[2,4,4,32,1024]{4,3,2,1,0:T(8,128)(2,1)} %get-tuple-element.163) | copy-start | bytes 6291460
  242.6 6.1 %copy-start.93 = (bf16[1024,1024]{1,0:T(8,128)(2,1)S(1)}, bf16[1024,1024]{1,0:T(8,128)(2,1)}, u32[]{:S(2)}) copy-start(bf16[1024,1024]{1,0:T(8,128)(2,1)} %get-tuple-element.280) | copy-start | bytes 6291460
  271.4 5.3 copy-start.10
  271.4 5.3 copy-start.39
  271.4 5.3 copy-start.41
  276.6 19.6 %slice-start.2 = ((s8[8388608]{0:T(1024)(128)(4,1)}), s8[4194304]{0:T(1024)(128)(4,1)S(1)}, s32[]{:S(2)}) async-start(s8[8388608]{0:T(1024)(128)(4,1)} %bitcast.261), calls=%async_computation.2 | async-start | bytes 8388608
  278.2 18.0 %slice-start.3 = ((s8[8388608]{0:T(1024)(128)(4,1)}), s8[4194304]{0:T(1024)(128)(4,1)S(1)}, s32[]{:S(2)}) async-start(s8[8388608]{0:T(1024)(128)(4,1)} %bitcast.261), calls=%async_computation.3 | async-start | bytes 8388608
  305.6 5.1 copy-start.48
  305.6 5.2 copy-start.49
  313.8 19.9 %copy-start.66 = (f32[1024]{0:T(1024)S(1)}, f32[1024]{0:T(1024)}, u32[]{:S(2)}) copy-start(f32[1024]{0:T(1024)} %copy-done.65) | copy-start | bytes 12292
  313.8 19.9 %copy-start.72 = (f32[256]{0:T(256)S(1)}, f32[256]{0:T(256)}, u32[]{:S(2)}) copy-start(f32[256]{0:T(256)} %copy-done.71) | copy-start | bytes 3076
  313.8 19.9 %copy-start.74 = (f32[256]{0:T(256)S(1)}, f32[256]{0:T(256)}, u32[]{:S(2)}) copy-start(f32[256]{0:T(256)} %copy-done.73) | copy-start | bytes 3076
  313.8 21.6 %copy-start.78 = (f32[1024]{0:T(1024)S(1)}, f32[1024]{0:T(1024)}, u32[]{:S(2)}) copy-start(f32[1024]{0:T(1024)} %add.285) | copy-start | bytes 12292
  316.4 19.0 %copy-start.5 = (f32[256,1024]{1,0:T(8,128)S(1)}, f32[256,1024]{1,0:T(8,128)}, u32[]{:S(2)}) copy-start(f32[256,1024]{1,0:T(8,128)} %copy-done.4) | copy-start | bytes 3145732
  316.4 19.0 %copy-start.15 = (bf16[256,1024]{1,0:T(8,128)(2,1)S(1)}, bf16[256,1024]{1,0:T(8,128)(2,1)}, u32[]{:S(2)}) copy-start(bf16[256,1024]{1,0:T(8,128)(2,1)} %own) | copy-start | bytes 1572868
  335.4 24.8 %copy-start.35 = (bf16[32,8,512]{2,1,0:T(8,128)(2,1)S(1)}, bf16[32,8,512]{2,1,0:T(8,128)(2,1)}, u32[]{:S(2)}) copy-start(bf16[32,8,512]{2,1,0:T(8,128)(2,1)} %copy-done.34) | copy-start | bytes 786436
  335.4 24.8 %copy-start.37 = (bf16[32,8,512]{2,1,0:T(8,128)(2,1)S(1)}, bf16[32,8,512]{2,1,0:T(8,128)(2,1)}, u32[]{:S(2)}) copy-start(bf16[32,8,512]{2,1,0:T(8,128)(2,1)} %copy-done.36) | copy-start | bytes 786436
  336.8 25.9 %copy-start.8 = (f32[256,1024]{1,0:T(8,128)}, f32[256,1024]{1,0:T(8,128)S(1)}, u32[]{:S(2)}) copy-start(f32[256,1024]{1,0:T(8,128)S(1)} %get-tuple-element.194) | copy-start | bytes 3145732
  338.7 24.0 %copy-start.52 = (bf16[4,64,512]{2,1,0:T(8,128)(2,1)S(1)}, bf16[4,64,512]{2,1,0:T(8,128)(2,1)}, u32[]{:S(2)}) copy-start(bf16[4,64,512]{2,1,0:T(8,128)(2,1)} %copy-done.51) | copy-start | bytes 786436
  338.7 24.0 %copy-start.54 = (bf16[4,64,512]{2,1,0:T(8,128)(2,1)S(1)}, bf16[4,64,512]{2,1,0:T(8,128)(2,1)}, u32[]{:S(2)}) copy-start(bf16[4,64,512]{2,1,0:T(8,128)(2,1)} %copy-done.53) | copy-start | bytes 786436
  360.2 6.0 %copy-start.91 = (f32[1024,1024]{1,0:T(8,128)S(1)}, f32[1024,1024]{1,0:T(8,128)}, u32[]{:S(2)}) copy-start(f32[1024,1024]{1,0:T(8,128)} %copy-done.90) | copy-start | bytes 12582916
  372.5 5.4 copy-start.61
  380.8 6.0 %copy-start.17 = (bf16[4,256,1024]{2,1,0:T(8,128)(2,1)S(1)}, bf16[4,256,1024]{2,1,0:T(8,128)(2,1)}, u32[]{:S(2)}) copy-start(bf16[4,256,1024]{2,1,0:T(8,128)(2,1)} %gather_rows.4) | copy-start | bytes 6291460
  386.9 5.4 %copy-start.83 = (bf16[2,4,4,32,1024]{4,3,2,1,0:T(8,128)(2,1)S(1)}, bf16[2,4,4,32,1024]{4,3,2,1,0:T(8,128)(2,1)}, u32[]{:S(2)}) copy-start(bf16[2,4,4,32,1024]{4,3,2,1,0:T(8,128)(2,1)} %get-tuple-element.159) | copy-start | bytes 6291460
  386.9 5.4 %copy-start.92 = (bf16[1024,1024]{1,0:T(8,128)(2,1)S(1)}, bf16[1024,1024]{1,0:T(8,128)(2,1)}, u32[]{:S(2)}) copy-start(bf16[1024,1024]{1,0:T(8,128)(2,1)} %get-tuple-element.196) | copy-start | bytes 6291460
  417.8 19.7 %copy-start.7 = (bf16[256,1024]{1,0:T(8,128)(2,1)S(1)}, bf16[256,1024]{1,0:T(8,128)(2,1)}, u32[]{:S(2)}) copy-start(bf16[256,1024]{1,0:T(8,128)(2,1)} %param.35) | copy-start | bytes 1572868
  417.8 19.7 %copy-start.63 = (f32[1024]{0:T(1024)S(1)}, f32[1024]{0:T(1024)}, u32[]{:S(2)}) copy-start(f32[1024]{0:T(1024)} %copy-done.62) | copy-start | bytes 12292
  417.8 19.7 %copy-start.70 = (f32[256]{0:T(256)S(1)}, f32[256]{0:T(256)}, u32[]{:S(2)}) copy-start(f32[256]{0:T(256)} %copy-done.69) | copy-start | bytes 3076
  417.8 19.7 %copy-start.77 = (f32[256]{0:T(256)S(1)}, f32[256]{0:T(256)}, u32[]{:S(2)}) copy-start(f32[256]{0:T(256)} %copy-done.76) | copy-start | bytes 3076
  420.7 17.4 %copy-start.9 = (f32[256,1024]{1,0:T(8,128)S(1)}, f32[256,1024]{1,0:T(8,128)}, u32[]{:S(2)}) copy-start(f32[256,1024]{1,0:T(8,128)} %copy-done.8) | copy-start | bytes 3145732
  420.7 18.9 %copy-start.59 = (f32[1,32,4,8]{3,2,1,0:T(4,128)S(1)}, f32[1,32,4,8]{3,2,1,0:T(4,128)}, u32[]{:S(2)}) copy-start(f32[1,32,4,8]{3,2,1,0:T(4,128)} %stack.105) | copy-start | bytes 12292
  420.7 19.2 %copy-start.60 = (f32[1,32,4,8]{3,2,1,0:T(4,128)S(1)}, f32[1,32,4,8]{3,2,1,0:T(4,128)}, u32[]{:S(2)}) copy-start(f32[1,32,4,8]{3,2,1,0:T(4,128)} %stack.108) | copy-start | bytes 12292
  420.7 19.5 %copy-start.57 = (f32[32,4,64]{2,1,0:T(4,128)S(1)}, f32[32,4,64]{2,1,0:T(4,128)}, u32[]{:S(2)}) copy-start(f32[32,4,64]{2,1,0:T(4,128)} %broadcast_select_fusion) | copy-start | bytes 98308
  420.8 19.5 %copy-start.58 = (f32[32,4,16]{2,1,0:T(4,128)S(1)}, f32[32,4,16]{2,1,0:T(4,128)}, u32[]{:S(2)}) copy-start(f32[32,4,16]{2,1,0:T(4,128)} %copy.120) | copy-start | bytes 24580
  (50 other events, 154.2 us)
